TPU v7x, 32 devices: a whole 2x2x4 slice. The times are simulated.
32 devices in a mesh: groups: 2 (over x), slab: 16 (over z, y, core).
Axes of the slice: x: 2, y: 2, z: 4, core: 2. Of those that a mesh axis runs over, the one named last changes fastest.
Arguments:
- latent: bfloat16 [64, 32, 2048], P(None, ('groups', 'slab')), parts along dimension 1, may hold values from -6 to 6
- conv1_weight: bfloat16 [27, 64, 64], replicated, may hold values from -0.15625 to 0.15625
- conv2_weight: bfloat16 [27, 64, 64], replicated, may hold values from -0.15625 to 0.15625
- head: bfloat16 [64], replicated, may hold values from -2 to 2
- p_prev: float32 [32, 16, 64, 128], P(('groups', 'slab')), parts along dimension 0, may hold values from -6 to 6
- p_cur: float32 [32, 16, 64, 128], P(('groups', 'slab')), parts along dimension 0, may hold values from -6 to 6
- adjoint: bfloat16 [4, 32, 16, 64, 128], P(None, ('groups', 'slab')), parts along dimension 1, may hold values from -6 to 6
- wavelet: float32 [16, 4], P('groups'), parts along dimension 0, may hold values from -12 to 12
- sources: int32 [16, 3], P('groups'), parts along dimension 0, may hold values from 0 to 127, as said below
- receivers: int32 [16, 3, 128], P('groups'), parts along dimension 0, may hold values from 0 to 127, as said below
Outputs:
- pressure_final: float32 [32, 16, 64, 128], P(('groups', 'slab')), parts along dimension 0
- traces: float32 [16, 4, 128], P('groups'), parts along dimension 0
- gradient: float32 [32, 2048], P(('groups', 'slab')), parts along dimension 0
There are 2 independent parts, one for each index of `groups`. A program takes and returns all parts, laid end to end along the dimension named above; an argument that names none is the same for every part. Nothing has to cross between parts.
Inputs may be any that keep to these rules, and one draw needn't show every extreme that they name: sources[s] is the source cell (depth, row, column) of shot s on the fine grid: depth below 32, row below 64, column below 128. receivers[s, :, k] is the cell (depth, row, column) of receiver k of shot s on the fine grid: depth below 32, row below 64, column below 128.
All inputs are finite; a program needn't handle non-finite values.
Results may differ from a plain program's by a relative error of at most 0.006.
Values may be sent and summed in bfloat16 or wider, within the bound.
A program may use at most 64 MiB of HBM per device.

v0:
```python
import jax
import jax.numpy as jnp
from jax import lax
from jax.sharding import PartitionSpec as P

CY = 32
CX = 64
SHOTS = 8
STEPS = 4
stencil_weights = (-205.0 / 72.0, 8.0 / 5.0, -1.0 / 5.0, 8.0 / 315.0, -1.0 / 560.0)
lowest_speed = 1.5
speed_range = 3.0
courant = 0.088
leak_slope = 0.2


def extended_2(block, sides, width):
    for axis, dim in sides:
        count = lax.axis_size(axis)
        forward = [(i, i + 1) for i in range(count - 1)]
        backward = [(target, source) for source, target in forward]
        low = lax.ppermute(
            lax.slice_in_dim(block, block.shape[dim] - width, None, axis=dim), axis, forward
        )
        high = lax.ppermute(lax.slice_in_dim(block, 0, width, axis=dim), axis, backward)
        block = jnp.concatenate([low, block, high], axis=dim)
    return block


def from_partner(value, axis, apart):
    mask = 2**apart
    pairs = [(source, source ^ mask) for source in range(lax.axis_size(axis))]
    return lax.ppermute(value, axis, pairs)


def for_sending(shard):
    return jax.tree.map(lambda a: a.astype(jnp.bfloat16) if a.dtype == jnp.float32 else a, shard)


def from_behind(value, axis, steps):
    count = lax.axis_size(axis)
    leading, last = (max(0, -steps), min(count, count - steps))
    return lax.ppermute(value, axis, [(source, source + steps) for source in range(leading, last)])


def conv_taps(extended_in, weight):
    planes = extended_in.shape[1] - 2
    cell_count = extended_in.shape[2]
    extended = jnp.pad(extended_in, ((0, 0), (0, 0), (CX + 1, CX + 1)))
    columns = jnp.arange(cell_count) % CX
    accumulated = jnp.zeros((weight.shape[1], planes, cell_count), jnp.float32)
    tap_index = 0
    for depth_off in range(3):
        for row_off in (-1, 0, 1):
            for col_off in (-1, 0, 1):
                begin_at = CX + 1 + row_off * CX + col_off
                piece = extended[
                    :, depth_off : depth_off + planes, begin_at : begin_at + cell_count
                ]
                column_valid = ((columns + col_off >= 0) & (columns + col_off < CX)).astype(
                    extended.dtype
                )
                accumulated = accumulated + jnp.einsum(
                    "oi,izn->ozn",
                    weight[tap_index],
                    piece * column_valid,
                    preferred_element_type=jnp.float32,
                )
                tap_index += 1
    return accumulated


def double_axis(values, axis):
    length = values.shape[axis]
    lower_side = jnp.concatenate(
        [
            lax.slice_in_dim(values, 0, 1, axis=axis),
            lax.slice_in_dim(values, 0, length - 1, axis=axis),
        ],
        axis=axis,
    )
    upper_side = jnp.concatenate(
        [
            lax.slice_in_dim(values, 1, length, axis=axis),
            lax.slice_in_dim(values, length - 1, length, axis=axis),
        ],
        axis=axis,
    )
    even_part = 0.75 * values + 0.25 * lower_side
    odd_part = 0.75 * values + 0.25 * upper_side
    new_shape = list(values.shape)
    new_shape[axis] = 2 * length
    return jnp.stack([even_part, odd_part], axis=axis + 1).reshape(new_shape)


def double_depth(rimmed):
    inner_planes = rimmed.shape[0] - 2
    middle = rimmed[1:-1]
    even_part = 0.75 * middle + 0.25 * rimmed[:-2]
    odd_part = 0.75 * middle + 0.25 * rimmed[2:]
    return jnp.stack([even_part, odd_part], axis=1).reshape((2 * inner_planes,) + rimmed.shape[1:])


def upsample_slab(rimmed):
    deeper = double_depth(rimmed).reshape(2 * (rimmed.shape[0] - 2), CY, CX)
    return double_axis(double_axis(deeper, 1), 2)


def stencil(extended):
    depth_total = extended.shape[0] - 8
    row_total = extended.shape[1]
    col_total = extended.shape[2]
    padded = jnp.pad(extended, ((0, 0), (4, 4), (4, 4)))

    def window(depth_at, row_at, col_at):
        return padded[
            depth_at : depth_at + depth_total,
            row_at : row_at + row_total,
            col_at : col_at + col_total,
        ]

    accumulated = 3.0 * stencil_weights[0] * window(4, 4, 4)
    for reach in range(1, 5):
        near_sum = window(4 - reach, 4, 4) + window(4 + reach, 4, 4)
        near_sum = near_sum + window(4, 4 - reach, 4) + window(4, 4 + reach, 4)
        near_sum = near_sum + window(4, 4, 4 - reach) + window(4, 4, 4 + reach)
        accumulated = accumulated + stencil_weights[reach] * near_sum
    return accumulated


def body(
    latent, conv1_weight, conv2_weight, head, p_prev, p_cur, adjoint, wavelet, sources, receivers
):
    position = lax.axis_index("slab")
    devices = lax.axis_size("slab")
    my_shot = position % SHOTS
    slab_index = position // SHOTS
    slab_total = devices // SHOTS
    group_bits = SHOTS.bit_length() - 1
    latent_wide = extended_2(latent, (("slab", 1),), 1)
    hidden = jax.nn.leaky_relu(conv_taps(latent_wide, conv1_weight), leak_slope).astype(
        jnp.bfloat16
    )
    hidden_wide = extended_2(hidden, (("slab", 1),), 1)
    second = jax.nn.leaky_relu(conv_taps(hidden_wide, conv2_weight), leak_slope)
    logits = jnp.einsum(
        "c,czn->zn", head.astype(jnp.float32), second, precision=lax.Precision.HIGHEST
    )
    velocity = (lowest_speed + speed_range * jax.nn.sigmoid(logits)).astype(jnp.bfloat16)
    planes = velocity.shape[0]
    slab_planes = planes * SHOTS
    rimmed = extended_2(velocity, (("slab", 0),), 1)
    rimmed = jnp.concatenate(
        [
            jnp.where(position == 0, velocity, rimmed[:1]),
            rimmed[1:-1],
            jnp.where(position == devices - 1, velocity, rimmed[-1:]),
        ],
        axis=0,
    )
    tile_doubled = double_depth(rimmed.astype(jnp.float32))
    bit_order = list(range(group_bits))
    blocks = tile_doubled[None]
    for bit_index in bit_order:
        partner = from_partner(blocks, "slab", bit_index)
        upper_bit = my_shot // (1 << bit_index) % 2 == 1
        blocks = jnp.where(
            upper_bit,
            jnp.concatenate([partner, blocks], axis=0),
            jnp.concatenate([blocks, partner], axis=0),
        )
    placed = []
    for shot_number in range(SHOTS):
        list_index = 0
        for section_number in range(group_bits):
            list_index = list_index + (
                (shot_number >> bit_order[section_number] & 1) << section_number
            )
        placed.append(blocks[list_index])
    deeper = jnp.concatenate(placed, axis=0).reshape(2 * slab_planes, CY, CX)
    fine_speed = double_axis(double_axis(deeper, 1), 2)
    courant_sq = (courant * fine_speed) ** 2
    previous = p_prev[0]
    current = p_cur[0]
    fine_planes = current.shape[0]
    offset = slab_index * fine_planes
    source = lax.dynamic_index_in_dim(sources, my_shot, 0, keepdims=False)
    station = lax.dynamic_index_in_dim(receivers, my_shot, 0, keepdims=False)
    pulses = lax.dynamic_index_in_dim(wavelet, my_shot, 0, keepdims=False)
    source_depth = source[0] - offset
    source_inside = (source_depth >= 0) & (source_depth < fine_planes)
    source_depth = jnp.clip(source_depth, 0, fine_planes - 1)
    station_depth = station[0] - offset
    station_inside = (station_depth >= 0) & (station_depth < fine_planes)
    station_depth = jnp.clip(station_depth, 0, fine_planes - 1)
    correlation = jnp.zeros(current.shape, jnp.float32)
    samples_list = []
    for step_index in range(STEPS):
        rim_below = from_behind(for_sending(current[-4:]), "slab", SHOTS)
        rim_above = from_behind(for_sending(current[:4]), "slab", -SHOTS)
        laplace_term = stencil(jnp.concatenate([rim_below, current, rim_above], axis=0))
        correlation = correlation + adjoint[step_index, 0].astype(jnp.float32) * laplace_term
        advanced = 2.0 * current - previous + courant_sq * laplace_term
        advanced = advanced.at[source_depth, source[1], source[2]].add(
            jnp.where(source_inside, pulses[step_index], 0.0)
        )
        samples_list.append(
            jnp.where(station_inside, advanced[station_depth, station[1], station[2]], 0.0)
        )
        previous, current = (current, advanced)
    record = jnp.stack(samples_list)
    own_traces = jnp.where((jnp.arange(SHOTS) == my_shot)[:, None, None], record[None], 0.0)
    traces = lax.psum(own_traces, "slab")
    fine_gradient = 2.0 * courant * courant * fine_speed * correlation
    shape_holder = jnp.zeros((slab_planes + 2, velocity.shape[1]), jnp.float32)
    unused, pullback = jax.vjp(upsample_slab, shape_holder)
    grad_rim = pullback(fine_gradient)[0]
    first_slab = slab_index == 0
    last_slab = slab_index == slab_total - 1
    folded = jnp.concatenate(
        [
            jnp.where(first_slab, 0.0, grad_rim[:1]),
            grad_rim[1:2] + jnp.where(first_slab, grad_rim[:1], 0.0),
            grad_rim[2:-2],
            grad_rim[-2:-1] + jnp.where(last_slab, grad_rim[-1:], 0.0),
            jnp.where(last_slab, 0.0, grad_rim[-1:]),
        ],
        axis=0,
    )
    from_lower = from_behind(folded[-1:], "slab", SHOTS)
    from_upper = from_behind(folded[:1], "slab", -SHOTS)
    inner = folded[1:-1]
    inner = jnp.concatenate([inner[:1] + from_lower, inner[1:-1], inner[-1:] + from_upper], axis=0)
    blocks = inner.reshape(SHOTS, planes, inner.shape[1])
    for bit_index in reversed(range(group_bits)):
        halfway = blocks.shape[0] // 2
        upper_bit = my_shot // (1 << bit_index) % 2 == 1
        retained = jnp.where(upper_bit, blocks[halfway:], blocks[:halfway])
        outgoing = jnp.where(upper_bit, blocks[:halfway], blocks[halfway:])
        blocks = retained + from_partner(outgoing, "slab", bit_index)
    gradient = blocks[0]
    return (current[None], traces, gradient)


def solution(mesh):
    in_specs = (
        P(None, ("groups", "slab"), None),
        P(),
        P(),
        P(),
        P(("groups", "slab"), None, None, None),
        P(("groups", "slab"), None, None, None),
        P(None, ("groups", "slab"), None, None, None),
        P("groups", None),
        P("groups", None),
        P("groups", None, None),
    )
    out_specs = (
        P(("groups", "slab"), None, None, None),
        P("groups", None, None),
        P(("groups", "slab"), None),
    )
    return jax.shard_map(body, mesh=mesh, in_specs=in_specs, out_specs=out_specs, check_vma=False)
```

profile of v0, /device:TPU:0, one launch (start us, length us, event | category | flops | bytes accessed | tf_op | source)
XLA Modules:
  0.0 228.8 jit_solution(11264955654170186735)
XLA Ops:
  2.1 3.1 %collective-permute-start = (bf16[64,1,2048]{2,0,1:T(8,128)(2,1)}, bf16[64,1,2048]{2,0,1:T(8,128)(2,1)S(1)}, u32[]{:S(2)}, u32[]{:S(2)}) collective-permute-start(bf16[64,1,2048]{2,0,1:T(8,128)(2,1)} %param.18), channel_id=1, source_target_pairs={{0,1},{1,2},{2,3},{3,4},{4,5},{5,6},{6,7},{7,8},{8,9},{9,10},{10,1... | collective-permute-start | bytes 786440 | tf_op jit(solution)/shard_map/ppermute | solution.py:22
  16.5 9.2 %collective-permute-start.2 = (bf16[64,1,2048]{2,0,1:T(8,128)(2,1)S(1)}, bf16[64,1,2048]{2,0,1:T(8,128)(2,1)S(1)}, u32[]{:S(2)}, u32[]{:S(2)}) collective-permute-start(bf16[64,1,2048]{2,0,1:T(8,128)(2,1)S(1)} %bitcast.577), channel_id=1, source_target_pairs={{0,1},{1,2},{2,3},{3,4},{4,5},{5,6},{6,7},{7,8},{8,9},{9,10},{10,1... | collective-permute-start | bytes 786440 | tf_op jit(solution)/shard_map/ppermute | solution.py:22
  25.7 5.7 %collective-permute-start.9 = (bf16[4,64,128]{2,1,0:T(8,128)(2,1)S(1)}, bf16[4,64,128]{2,1,0:T(8,128)(2,1)S(1)}, u32[]{:S(2)}, u32[]{:S(2)}) collective-permute-start(bf16[4,64,128]{2,1,0:T(8,128)(2,1)S(1)} %get-tuple-element.81), channel_id=1, source_target_pairs={{0,8},{1,9},{2,10},{3,11},{4,12},{5,13},{6,14},{7,15},{16,24},{17,... | collective-permute-start | bytes 196616 | tf_op jit(solution)/shard_map/ppermute | solution.py:43
  42.9 3.6 %collective-permute-start.4 = (bf16[1,2048]{1,0:T(2,128)(2,1)S(1)}, bf16[1,2048]{1,0:T(2,128)(2,1)S(1)}, u32[]{:S(2)}, u32[]{:S(2)}) collective-permute-start(bf16[1,2048]{1,0:T(2,128)(2,1)S(1)} %convert_element_type.266), channel_id=1, source_target_pairs={{0,1},{1,2},{2,3},{3,4},{4,5},{5,6},{6,7},{7,8},{8,9},{9,10},{10,1... | collective-permute-start | bytes 12296 | tf_op jit(solution)/shard_map/ppermute | solution.py:22
  47.4 1.8 collective-permute-start.6
  54.2 2.4 %collective-permute-start.7 = (f32[2,2,2048]{2,1,0:T(2,128)S(1)}, f32[2,2,2048]{2,1,0:T(2,128)S(1)}, u32[]{:S(2)}, u32[]{:S(2)}) collective-permute-start(f32[2,2,2048]{2,1,0:T(2,128)S(1)} %maximum_select_fusion.2), channel_id=1, source_target_pairs={{0,2},{1,3},{2,0},{3,1},{4,6},{5,7},{6,4},{7,5},{8,10},{9,11},{10,... | collective-permute-start | bytes 98312 | tf_op jit(solution)/shard_map/ppermute | solution.py:33
  60.1 2.2 collective-permute-start.8
  62.8 1.7 collective-permute-done.8
  72.2 1.7 fusion.155
  75.1 1.9 copy.58
  77.0 1.6 copy.59
  78.6 4.4 %fusion.164 = (f32[16,64,128]{2,1,0:T(8,128)S(1)}, f32[16,64,128]{2,1,0:T(8,128)}) fusion(f32[1,16,64,128]{3,2,1,0:T(8,128)} %param.22, f32[16,64,128]{2,1,0:T(8,128)S(1)} %copy.59, f32[1,16,64,128]{3,2,1,0:T(8,128)S(1)} %copy-done.2, f32[24,72,136]{2,1,0:T(8,128)S(1)} %select_maximum_fusion.6, f32[4,64,128]{2,1,0:T(8,128)} %copy-done.11, ...), kind=kLoop, calls=%fused_computation.321 | loop fusion | flops 5373952 | bytes 11796480 | tf_op jit(solution)/shard_map/add | solution.py:203
  85.7 5.2 %collective-permute-start.11 = (bf16[4,64,128]{2,1,0:T(8,128)(2,1)S(1)}, bf16[4,64,128]{2,1,0:T(8,128)(2,1)S(1)}, u32[]{:S(2)}, u32[]{:S(2)}) collective-permute-start(bf16[4,64,128]{2,1,0:T(8,128)(2,1)S(1)} %get-tuple-element.79), channel_id=1, source_target_pairs={{0,8},{1,9},{2,10},{3,11},{4,12},{5,13},{6,14},{7,15},{16,24},{17,... | collective-permute-start | bytes 196616 | tf_op jit(solution)/shard_map/ppermute | solution.py:43
  92.7 5.2 %collective-permute-done.12 = bf16[4,64,128]{2,1,0:T(8,128)(2,1)S(1)} collective-permute-done((bf16[4,64,128]{2,1,0:T(8,128)(2,1)S(1)}, bf16[4,64,128]{2,1,0:T(8,128)(2,1)S(1)}, u32[]{:S(2)}, u32[]{:S(2)}) %collective-permute-start.12) | collective-permute-done | bytes 65568 | tf_op jit(solution)/shard_map/ppermute | solution.py:43
  99.1 4.2 %multiply_add_fusion.2 = (f32[16,64,128]{2,1,0:T(8,128)S(1)}, f32[16,64,128]{2,1,0:T(8,128)}) fusion(f32[16,64,128]{2,1,0:T(8,128)} %copy-done.3, f32[16,64,128]{2,1,0:T(8,128)S(1)} %scatter-add.14, f32[1,16,64,128]{3,2,1,0:T(8,128)S(1)} %copy-done.2, f32[24,72,136]{2,1,0:T(8,128)S(1)} %select_maximum_fusion.4, f32[4,64,128]{2,1,0:T(8,128)} %copy-done.13, ...), kind=kLoop, calls=%fused_computation.326 | loop fusion | flops 5373952 | bytes 11272192 | tf_op jit(solution)/shard_map/add | solution.py:203
  106.1 1.6 collective-permute-start.13
  107.7 1.5 collective-permute-start.14
  110.0 1.5 gather_fusion
  111.5 3.3 %collective-permute-done.14 = bf16[4,64,128]{2,1,0:T(8,128)(2,1)S(1)} collective-permute-done((bf16[4,64,128]{2,1,0:T(8,128)(2,1)S(1)}, bf16[4,64,128]{2,1,0:T(8,128)(2,1)S(1)}, u32[]{:S(2)}, u32[]{:S(2)}) %collective-permute-start.14) | collective-permute-done | bytes 65568 | tf_op jit(solution)/shard_map/ppermute | solution.py:43
  116.0 4.2 %multiply_add_fusion.1 = (f32[16,64,128]{2,1,0:T(8,128)S(1)}, f32[16,64,128]{2,1,0:T(8,128)}) fusion(f32[16,64,128]{2,1,0:T(8,128)} %copy-done.3, f32[16,64,128]{2,1,0:T(8,128)S(1)} %scatter-add.14, f32[16,64,128]{2,1,0:T(8,128)S(1)} %scatter-add.15, f32[24,72,136]{2,1,0:T(8,128)S(1)} %select_maximum_fusion.2, f32[4,64,128]{2,1,0:T(8,128)} %copy-done.12, ...), kind=kLoop, calls=%fused_computation.325 | loop fusion | flops 5373952 | bytes 11272192 | tf_op jit(solution)/shard_map/add | solution.py:203
  123.0 2.2 collective-permute-start.15
  127.2 2.0 copy.63
  129.2 2.4 %copy.64 = f32[16,64,128]{2,1,0:T(8,128)} copy(f32[16,64,128]{1,0,2:T(8,128)} %bitcast.569) | data formatting | bytes 1048576 | tf_op jit(solution)/shard_map/mul | solution.py:214
  136.0 3.4 %fusion.158 = (f32[16,64,128]{2,1,0:T(8,128)}, f32[16,64,128]{2,1,0:T(8,128)S(1)}) fusion(f32[16,64,128]{2,1,0:T(8,128)S(1)} %copy-done.10, f32[16,64,128]{2,1,0:T(8,128)S(1)} %copy-done.9, f32[16,64,128]{2,1,0:T(8,128)S(1)} %copy-done.8, f32[16,64,128]{2,1,0:T(8,128)S(1)} %copy-done.7, bf16[4,1,16,64,128]{4,3,2,1,0:T(8,128)(2,1)S(1)} %copy-done.14, ...), kind=kLoop, calls=%fused_computation.310 | loop fusion | flops 6422528 | bytes 13369344 | tf_op jit(solution)/shard_map/mul | solution.py:214
  143.7 1.5 copy.65
  148.5 5.4 %collective-permute-start.18 = (f32[1,2048]{1,0:T(1,128)S(1)}, f32[1,2048]{1,0:T(1,128)S(1)}, u32[]{:S(2)}, u32[]{:S(2)}) collective-permute-start(f32[1,2048]{1,0:T(1,128)S(1)} %get-tuple-element.91), channel_id=1, source_target_pairs={{0,8},{1,9},{2,10},{3,11},{4,12},{5,13},{6,14},{7,15},{16,24},{17,... | collective-permute-start | bytes 24584 | tf_op jit(solution)/shard_map/ppermute | solution.py:43
  155.3 5.1 %collective-permute-done.17 = f32[1,2048]{1,0:T(1,128)S(1)} collective-permute-done((f32[1,2048]{1,0:T(1,128)S(1)}, f32[1,2048]{1,0:T(1,128)S(1)}, u32[]{:S(2)}, u32[]{:S(2)}) %collective-permute-start.17) | collective-permute-done | bytes 8224 | tf_op jit(solution)/shard_map/ppermute | solution.py:43
  160.5 2.1 collective-permute-start.19
  162.6 1.9 collective-permute-done.19
  164.5 1.8 collective-permute-start.20
  166.4 2.0 collective-permute-done.20
  168.4 59.7 %psum.7 = f32[8,4,128]{2,1,0:T(4,128)} all-reduce(f32[8,4,128]{2,1,0:T(4,128)S(1)} %broadcast_select_fusion.9), channel_id=1, replica_groups=mesh['groups'=2,'slab'=16] {'slab'}, use_global_device_ids=true, to_apply=%region_1.2 | all-reduce | flops 4096 | bytes 32768 | tf_op jit(solution)/shard_map/psum | solution.py:213
  (255 shorter events, 56.6 us)
Async XLA Ops:
  0.6 32.1 %copy-start = (f32[8,4]{0,1:T(4,128)S(1)}, f32[8,4]{0,1:T(4,128)}, u32[]{:S(2)}) copy-start(f32[8,4]{0,1:T(4,128)} %param.25) | copy-start | bytes 388
  0.6 7.1 %copy-start.17 = (bf16[27,64,64]{2,1,0:T(8,128)(2,1)S(1)}, bf16[27,64,64]{2,1,0:T(8,128)(2,1)}, u32[]{:S(2)}) copy-start(bf16[27,64,64]{2,1,0:T(8,128)(2,1)} %param.19) | copy-start | bytes 663556
  0.7 5.6 %collective-permute-start.1 = (bf16[64,1,2048]{2,0,1:T(8,128)(2,1)}, bf16[64,1,2048]{2,0,1:T(8,128)(2,1)S(1)}, u32[]{:S(2)}, u32[]{:S(2)}) collective-permute-start(bf16[64,1,2048]{2,0,1:T(8,128)(2,1)} %param.18), channel_id=1, source_target_pairs={{1,0},{2,1},{3,2},{4,3},{5,4},{6,5},{7,6},{8,7},{9,8},{10,9},{11,1... | collective-permute-start | bytes 786440 | tf_op jit(solution)/shard_map/ppermute | solution.py:25
  2.1 4.4 %collective-permute-start = (bf16[64,1,2048]{2,0,1:T(8,128)(2,1)}, bf16[64,1,2048]{2,0,1:T(8,128)(2,1)S(1)}, u32[]{:S(2)}, u32[]{:S(2)}) collective-permute-start(bf16[64,1,2048]{2,0,1:T(8,128)(2,1)} %param.18), channel_id=1, source_target_pairs={{0,1},{1,2},{2,3},{3,4},{4,5},{5,6},{6,7},{7,8},{8,9},{9,10},{10,1... | collective-permute-start | bytes 786440 | tf_op jit(solution)/shard_map/ppermute | solution.py:22
  14.9 19.0 %copy-start.16 = (bf16[27,64,64]{2,1,0:T(8,128)(2,1)S(1)}, bf16[27,64,64]{2,1,0:T(8,128)(2,1)}, u32[]{:S(2)}) copy-start(bf16[27,64,64]{2,1,0:T(8,128)(2,1)} %param.20) | copy-start | bytes 663556
  15.2 18.2 %collective-permute-start.3 = (bf16[64,1,2048]{2,0,1:T(8,128)(2,1)S(1)}, bf16[64,1,2048]{2,0,1:T(8,128)(2,1)S(1)}, u32[]{:S(2)}, u32[]{:S(2)}) collective-permute-start(bf16[64,1,2048]{2,0,1:T(8,128)(2,1)S(1)} %bitcast.576), channel_id=1, source_target_pairs={{1,0},{2,1},{3,2},{4,3},{5,4},{6,5},{7,6},{8,7},{9,8},{10,9},{11,1... | collective-permute-start | bytes 786440 | tf_op jit(solution)/shard_map/ppermute | solution.py:25
  16.5 16.9 %collective-permute-start.2 = (bf16[64,1,2048]{2,0,1:T(8,128)(2,1)S(1)}, bf16[64,1,2048]{2,0,1:T(8,128)(2,1)S(1)}, u32[]{:S(2)}, u32[]{:S(2)}) collective-permute-start(bf16[64,1,2048]{2,0,1:T(8,128)(2,1)S(1)} %bitcast.577), channel_id=1, source_target_pairs={{0,1},{1,2},{2,3},{3,4},{4,5},{5,6},{6,7},{7,8},{8,9},{9,10},{10,1... | collective-permute-start | bytes 786440 | tf_op jit(solution)/shard_map/ppermute | solution.py:22
  25.7 34.2 %collective-permute-start.9 = (bf16[4,64,128]{2,1,0:T(8,128)(2,1)S(1)}, bf16[4,64,128]{2,1,0:T(8,128)(2,1)S(1)}, u32[]{:S(2)}, u32[]{:S(2)}) collective-permute-start(bf16[4,64,128]{2,1,0:T(8,128)(2,1)S(1)} %get-tuple-element.81), channel_id=1, source_target_pairs={{0,8},{1,9},{2,10},{3,11},{4,12},{5,13},{6,14},{7,15},{16,24},{17,... | collective-permute-start | bytes 196616 | tf_op jit(solution)/shard_map/ppermute | solution.py:43
  31.4 28.6 %collective-permute-start.10 = (bf16[4,64,128]{2,1,0:T(8,128)(2,1)S(1)}, bf16[4,64,128]{2,1,0:T(8,128)(2,1)S(1)}, u32[]{:S(2)}, u32[]{:S(2)}) collective-permute-start(bf16[4,64,128]{2,1,0:T(8,128)(2,1)S(1)} %get-tuple-element.82), channel_id=1, source_target_pairs={{8,0},{9,1},{10,2},{11,3},{12,4},{13,5},{14,6},{15,7},{24,16},{25,... | collective-permute-start | bytes 196616 | tf_op jit(solution)/shard_map/ppermute | solution.py:43
  40.7 5.9 %copy-start.18 = (s32[8,3]{0,1:T(4,128)S(1)}, s32[8,3]{0,1:T(4,128)}, u32[]{:S(2)}) copy-start(s32[8,3]{0,1:T(4,128)} %param.26) | copy-start | bytes 292
  40.7 16.0 %copy-start.21 = (s32[3]{0:T(128)S(1)}, s32[3]{0:T(128)}, u32[]{:S(2)}) copy-start(s32[3]{0:T(128)} %constant.246.clone.1) | copy-start | bytes 40
  40.7 21.6 %copy-start.2 = (f32[1,16,64,128]{3,2,1,0:T(8,128)S(1)}, f32[1,16,64,128]{3,2,1,0:T(8,128)}, u32[]{:S(2)}) copy-start(f32[1,16,64,128]{3,2,1,0:T(8,128)} %param.23) | copy-start | bytes 1572868
  41.6 5.0 %collective-permute-start.5 = (bf16[1,2048]{1,0:T(2,128)(2,1)S(1)}, bf16[1,2048]{1,0:T(2,128)(2,1)S(1)}, u32[]{:S(2)}, u32[]{:S(2)}) collective-permute-start(bf16[1,2048]{1,0:T(2,128)(2,1)S(1)} %convert_element_type.266), channel_id=1, source_target_pairs={{1,0},{2,1},{3,2},{4,3},{5,4},{6,5},{7,6},{8,7},{9,8},{10,9},{11,1... | collective-permute-start | bytes 12296 | tf_op jit(solution)/shard_map/ppermute | solution.py:25
  42.9 4.3 %collective-permute-start.4 = (bf16[1,2048]{1,0:T(2,128)(2,1)S(1)}, bf16[1,2048]{1,0:T(2,128)(2,1)S(1)}, u32[]{:S(2)}, u32[]{:S(2)}) collective-permute-start(bf16[1,2048]{1,0:T(2,128)(2,1)S(1)} %convert_element_type.266), channel_id=1, source_target_pairs={{0,1},{1,2},{2,3},{3,4},{4,5},{5,6},{6,7},{7,8},{8,9},{9,10},{10,1... | collective-permute-start | bytes 12296 | tf_op jit(solution)/shard_map/ppermute | solution.py:22
  47.4 6.8 %collective-permute-start.6 = (f32[1,2,2048]{2,1,0:T(2,128)S(1)}, f32[1,2,2048]{2,1,0:T(2,128)S(1)}, u32[]{:S(2)}, u32[]{:S(2)}) collective-permute-start(f32[1,2,2048]{2,1,0:T(2,128)S(1)} %pad_maximum_fusion.12), channel_id=1, source_target_pairs={{0,1},{1,0},{2,3},{3,2},{4,5},{5,4},{6,7},{7,6},{8,9},{9,8},{10,11... | collective-permute-start | bytes 49160 | tf_op jit(solution)/shard_map/ppermute | solution.py:33
  54.2 5.8 %collective-permute-start.7 = (f32[2,2,2048]{2,1,0:T(2,128)S(1)}, f32[2,2,2048]{2,1,0:T(2,128)S(1)}, u32[]{:S(2)}, u32[]{:S(2)}) collective-permute-start(f32[2,2,2048]{2,1,0:T(2,128)S(1)} %maximum_select_fusion.2), channel_id=1, source_target_pairs={{0,2},{1,3},{2,0},{3,1},{4,6},{5,7},{6,4},{7,5},{8,10},{9,11},{10,... | collective-permute-start | bytes 98312 | tf_op jit(solution)/shard_map/ppermute | solution.py:33
  60.0 5.3 %copy-start.11 = (f32[4,64,128]{2,1,0:T(8,128)}, f32[4,64,128]{2,1,0:T(8,128)S(1)}, u32[]{:S(2)}) copy-start(f32[4,64,128]{2,1,0:T(8,128)S(1)} %convert_element_type.271) | copy-start | bytes 393220
  60.1 4.5 %collective-permute-start.8 = (f32[4,2,2048]{2,1,0:T(2,128)S(1)}, f32[4,2,2048]{2,1,0:T(2,128)S(1)}, u32[]{:S(2)}, u32[]{:S(2)}) collective-permute-start(f32[4,2,2048]{2,1,0:T(2,128)S(1)} %maximum_select_fusion.1), channel_id=1, source_target_pairs={{0,4},{1,5},{2,6},{3,7},{4,0},{5,1},{6,2},{7,3},{8,12},{9,13},{10,... | collective-permute-start | bytes 196616 | tf_op jit(solution)/shard_map/ppermute | solution.py:33
  78.6 4.4 %copy-start.3 = (f32[16,64,128]{2,1,0:T(8,128)}, f32[16,64,128]{2,1,0:T(8,128)S(1)}, u32[]{:S(2)}) copy-start(f32[16,64,128]{2,1,0:T(8,128)S(1)} %copy.59) | copy-start | bytes 1572868
  85.7 7.1 %collective-permute-start.11 = (bf16[4,64,128]{2,1,0:T(8,128)(2,1)S(1)}, bf16[4,64,128]{2,1,0:T(8,128)(2,1)S(1)}, u32[]{:S(2)}, u32[]{:S(2)}) collective-permute-start(bf16[4,64,128]{2,1,0:T(8,128)(2,1)S(1)} %get-tuple-element.79), channel_id=1, source_target_pairs={{0,8},{1,9},{2,10},{3,11},{4,12},{5,13},{6,14},{7,15},{16,24},{17,... | collective-permute-start | bytes 196616 | tf_op jit(solution)/shard_map/ppermute | solution.py:43
  90.8 7.1 %collective-permute-start.12 = (bf16[4,64,128]{2,1,0:T(8,128)(2,1)S(1)}, bf16[4,64,128]{2,1,0:T(8,128)(2,1)S(1)}, u32[]{:S(2)}, u32[]{:S(2)}) collective-permute-start(bf16[4,64,128]{2,1,0:T(8,128)(2,1)S(1)} %get-tuple-element.80), channel_id=1, source_target_pairs={{8,0},{9,1},{10,2},{11,3},{12,4},{13,5},{14,6},{15,7},{24,16},{25,... | collective-permute-start | bytes 196616 | tf_op jit(solution)/shard_map/ppermute | solution.py:43
  106.1 5.3 %collective-permute-start.13 = (bf16[4,64,128]{2,1,0:T(8,128)(2,1)S(1)}, bf16[4,64,128]{2,1,0:T(8,128)(2,1)S(1)}, u32[]{:S(2)}, u32[]{:S(2)}) collective-permute-start(bf16[4,64,128]{2,1,0:T(8,128)(2,1)S(1)} %get-tuple-element.77), channel_id=1, source_target_pairs={{0,8},{1,9},{2,10},{3,11},{4,12},{5,13},{6,14},{7,15},{16,24},{17,... | collective-permute-start | bytes 196616 | tf_op jit(solution)/shard_map/ppermute | solution.py:43
  107.7 7.1 %collective-permute-start.14 = (bf16[4,64,128]{2,1,0:T(8,128)(2,1)S(1)}, bf16[4,64,128]{2,1,0:T(8,128)(2,1)S(1)}, u32[]{:S(2)}, u32[]{:S(2)}) collective-permute-start(bf16[4,64,128]{2,1,0:T(8,128)(2,1)S(1)} %get-tuple-element.78), channel_id=1, source_target_pairs={{8,0},{9,1},{10,2},{11,3},{12,4},{13,5},{14,6},{15,7},{24,16},{25,... | collective-permute-start | bytes 196616 | tf_op jit(solution)/shard_map/ppermute | solution.py:43
  120.1 7.1 %copy-start.5 = (f32[16,64,64,2]{2,0,1,3:T(8,128)S(1)}, f32[16,64,64,2]{2,0,1,3:T(8,128)}, u32[]{:S(2)}) copy-start(f32[16,64,64,2]{2,0,1,3:T(8,128)} %get-tuple-element.63) | copy-start | bytes 1572868
  123.0 11.6 %collective-permute-start.15 = (bf16[4,64,128]{2,1,0:T(8,128)(2,1)S(1)}, bf16[4,64,128]{2,1,0:T(8,128)(2,1)S(1)}, u32[]{:S(2)}, u32[]{:S(2)}) collective-permute-start(bf16[4,64,128]{2,1,0:T(8,128)(2,1)S(1)} %get-tuple-element.75), channel_id=1, source_target_pairs={{0,8},{1,9},{2,10},{3,11},{4,12},{5,13},{6,14},{7,15},{16,24},{17,... | collective-permute-start | bytes 196616 | tf_op jit(solution)/shard_map/ppermute | solution.py:43
  125.2 9.4 %collective-permute-start.16 = (bf16[4,64,128]{2,1,0:T(8,128)(2,1)S(1)}, bf16[4,64,128]{2,1,0:T(8,128)(2,1)S(1)}, u32[]{:S(2)}, u32[]{:S(2)}) collective-permute-start(bf16[4,64,128]{2,1,0:T(8,128)(2,1)S(1)} %get-tuple-element.76), channel_id=1, source_target_pairs={{8,0},{9,1},{10,2},{11,3},{12,4},{13,5},{14,6},{15,7},{24,16},{25,... | collective-permute-start | bytes 196616 | tf_op jit(solution)/shard_map/ppermute | solution.py:43
  147.4 81.3 %copy-start.1 = (f32[8,4]{0,1:T(4,128)S(1)}, f32[8,4]{0,1:T(4,128)}, u32[]{:S(2)}) copy-start(f32[8,4]{0,1:T(4,128)} %param.25) | copy-start | bytes 388
  148.5 6.8 %collective-permute-start.18 = (f32[1,2048]{1,0:T(1,128)S(1)}, f32[1,2048]{1,0:T(1,128)S(1)}, u32[]{:S(2)}, u32[]{:S(2)}) collective-permute-start(f32[1,2048]{1,0:T(1,128)S(1)} %get-tuple-element.91), channel_id=1, source_target_pairs={{0,8},{1,9},{2,10},{3,11},{4,12},{5,13},{6,14},{7,15},{16,24},{17,... | collective-permute-start | bytes 24584 | tf_op jit(solution)/shard_map/ppermute | solution.py:43
  153.9 6.4 %collective-permute-start.17 = (f32[1,2048]{1,0:T(1,128)S(1)}, f32[1,2048]{1,0:T(1,128)S(1)}, u32[]{:S(2)}, u32[]{:S(2)}) collective-permute-start(f32[1,2048]{1,0:T(1,128)S(1)} %get-tuple-element.92), channel_id=1, source_target_pairs={{8,0},{9,1},{10,2},{11,3},{12,4},{13,5},{14,6},{15,7},{24,16},{25,... | collective-permute-start | bytes 24584 | tf_op jit(solution)/shard_map/ppermute | solution.py:43
  160.5 4.0 %collective-permute-start.19 = (f32[4,1,2048]{2,0,1:T(4,128)S(1)}, f32[4,1,2048]{2,0,1:T(4,128)S(1)}, u32[]{:S(2)}, u32[]{:S(2)}) collective-permute-start(f32[4,1,2048]{2,0,1:T(4,128)S(1)} %select_bitcast_fusion), channel_id=1, source_target_pairs={{0,4},{1,5},{2,6},{3,7},{4,0},{5,1},{6,2},{7,3},{8,12},{9,13},{10,... | collective-permute-start | bytes 98312 | tf_op jit(solution)/shard_map/ppermute | solution.py:33
  164.5 3.8 %collective-permute-start.20 = (f32[2,1,2048]{2,0,1:T(2,128)S(1)}, f32[2,1,2048]{2,0,1:T(2,128)S(1)}, u32[]{:S(2)}, u32[]{:S(2)}) collective-permute-start(f32[2,1,2048]{2,0,1:T(2,128)S(1)} %broadcast_select_fusion.4), channel_id=1, source_target_pairs={{0,2},{1,3},{2,0},{3,1},{4,6},{5,7},{6,4},{7,5},{8,10},{9,11},{10,... | collective-permute-start | bytes 49160 | tf_op jit(solution)/shard_map/ppermute | solution.py:33
  168.3 59.8 %collective-permute-start.21 = (f32[1,1,2048]{2,0,1:T(1,128)S(1)}, f32[1,1,2048]{2,0,1:T(1,128)S(1)}, u32[]{:S(2)}, u32[]{:S(2)}) collective-permute-start(f32[1,1,2048]{2,0,1:T(1,128)S(1)} %broadcast_select_fusion.5), channel_id=1, source_target_pairs={{0,1},{1,0},{2,3},{3,2},{4,5},{5,4},{6,7},{7,6},{8,9},{9,8},{10,11... | collective-permute-start | bytes 24584 | tf_op jit(solution)/shard_map/ppermute | solution.py:33
  (13 other events, 19.8 us)
where the time goes:
time: 230 us; the launch traced here: 229 us
  blocking collectives  59.7 us (26%)
  starting transfers between devices  56.9 us (25%)
  local copies, waits for them, and re-layouts  31.1 us (14%)
  other arithmetic  28.9 us (13%)
  waiting for transfers between devices  20.4 us (9%)
  between operations  16.9 us (7%)
  matrix products  14.7 us (6%)
    psum x1, blocking collectives, body(): traces = lax.psum(own_traces, 'slab')  59.7 us
    ppermute x10, starting transfers between devices, from_behind(): lax.ppermute(value, axis, [(source, source + steps) for source in range(l...  26.7 us
    ppermute x3, starting transfers between devices, extended_2(): lax.ppermute(lax.slice_in_dim(block, block.shape[dim] - width, None, axis...  15.9 us
    dot_general x54, matrix products, conv_taps(): jnp.einsum('oi,izn->ozn', weight[tap_index], piece * column_valid, prefer...  14.4 us
    ppermute x10, waiting for transfers between devices, from_behind(): lax.ppermute(value, axis, [(source, source + steps) for source in range(l...  14.1 us
    add x4, other arithmetic, body(): advanced = 2.0 * current - previous + courant_sq * laplace_term  12.9 us
    ppermute x6, starting transfers between devices, from_partner(): return lax.ppermute(value, axis, pairs)  10.4 us
    gather x4, local copies, waits for them, and re-layouts, body(): advanced[station_depth, station[1], station[2]]  5.93 us
  transfers between devices with their start and end apart: 22, of which 9 were waited for; matrix products, arithmetic and copies ran while one was open for 10% of the time, Pallas kernels for 0%

commit v1 on v0

--- a/solution.py
+++ b/solution.py
@@ -210,7 +210,8 @@
         previous, current = (current, advanced)
     record = jnp.stack(samples_list)
     own_traces = jnp.where((jnp.arange(SHOTS) == my_shot)[:, None, None], record[None], 0.0)
-    traces = lax.psum(own_traces, "slab")
+    pieces = lax.all_gather(own_traces, "slab", axis=0, tiled=False)
+    traces = pieces.sum(axis=0)
     fine_gradient = 2.0 * courant * courant * fine_speed * correlation
     shape_holder = jnp.zeros((slab_planes + 2, velocity.shape[1]), jnp.float32)
     unused, pullback = jax.vjp(upsample_slab, shape_holder)

time: 230 us -> 191 us (0.83)
  blocking collectives: 59.7 us -> 19.9 us
    psum x1 -> x0, blocking collectives: 59.7 us -> none  [body(): traces = lax.psum(own_traces, 'slab')]
    all_gather x0 -> x1, blocking collectives: none -> 19.9 us  [body(): pieces = lax.all_gather(own_traces, 'slab', axis=0, tiled=False)]
  transfers between devices with their start and end apart: 22 -> 22, of which waited for: 9 -> 9; matrix products, arithmetic and copies ran while one was open for 10% -> 12% of each run, Pallas kernels for 0% -> 0%
where the time goes in v1:
time: 191 us; the launch traced here: 190 us
  starting transfers between devices  56.9 us (30%)
  local copies, waits for them, and re-layouts  31.8 us (17%)
  other arithmetic  28.9 us (15%)
  waiting for transfers between devices  20.4 us (11%)
  blocking collectives  19.9 us (10%)
  between operations  16.9 us (9%)
  matrix products  14.7 us (8%)
    ppermute x10, starting transfers between devices, from_behind(): lax.ppermute(value, axis, [(source, source + steps) for source in range(l...  26.7 us
    all_gather x1, blocking collectives, body(): pieces = lax.all_gather(own_traces, 'slab', axis=0, tiled=False)  19.9 us
    ppermute x3, starting transfers between devices, extended_2(): lax.ppermute(lax.slice_in_dim(block, block.shape[dim] - width, None, axis...  15.9 us
    dot_general x54, matrix products, conv_taps(): jnp.einsum('oi,izn->ozn', weight[tap_index], piece * column_valid, prefer...  14.4 us
    ppermute x10, waiting for transfers between devices, from_behind(): lax.ppermute(value, axis, [(source, source + steps) for source in range(l...  14.1 us
    add x4, other arithmetic, body(): advanced = 2.0 * current - previous + courant_sq * laplace_term  12.9 us
    ppermute x6, starting transfers between devices, from_partner(): return lax.ppermute(value, axis, pairs)  10.4 us
    gather x4, local copies, waits for them, and re-layouts, body(): advanced[station_depth, station[1], station[2]]  5.93 us
  transfers between devices with their start and end apart: 22, of which 9 were waited for; matrix products, arithmetic and copies ran while one was open for 12% of the time, Pallas kernels for 0%

profile of v1, /device:TPU:0, one launch (start us, length us, event | category | flops | bytes accessed | tf_op | source)
XLA Modules:
  0.0 189.6 jit_solution(3988379704570082587)
XLA Ops:
  2.1 3.1 %collective-permute-start = (bf16[64,1,2048]{2,0,1:T(8,128)(2,1)}, bf16[64,1,2048]{2,0,1:T(8,128)(2,1)S(1)}, u32[]{:S(2)}, u32[]{:S(2)}) collective-permute-start(bf16[64,1,2048]{2,0,1:T(8,128)(2,1)} %param.18), channel_id=1, source_target_pairs={{0,1},{1,2},{2,3},{3,4},{4,5},{5,6},{6,7},{7,8},{8,9},{9,10},{10,1... | collective-permute-start | bytes 786440 | tf_op jit(solution)/shard_map/ppermute | solution.py:22
  16.5 9.2 %collective-permute-start.2 = (bf16[64,1,2048]{2,0,1:T(8,128)(2,1)S(1)}, bf16[64,1,2048]{2,0,1:T(8,128)(2,1)S(1)}, u32[]{:S(2)}, u32[]{:S(2)}) collective-permute-start(bf16[64,1,2048]{2,0,1:T(8,128)(2,1)S(1)} %bitcast.577), channel_id=1, source_target_pairs={{0,1},{1,2},{2,3},{3,4},{4,5},{5,6},{6,7},{7,8},{8,9},{9,10},{10,1... | collective-permute-start | bytes 786440 | tf_op jit(solution)/shard_map/ppermute | solution.py:22
  25.7 5.7 %collective-permute-start.9 = (bf16[4,64,128]{2,1,0:T(8,128)(2,1)S(1)}, bf16[4,64,128]{2,1,0:T(8,128)(2,1)S(1)}, u32[]{:S(2)}, u32[]{:S(2)}) collective-permute-start(bf16[4,64,128]{2,1,0:T(8,128)(2,1)S(1)} %get-tuple-element.84), channel_id=1, source_target_pairs={{0,8},{1,9},{2,10},{3,11},{4,12},{5,13},{6,14},{7,15},{16,24},{17,... | collective-permute-start | bytes 196616 | tf_op jit(solution)/shard_map/ppermute | solution.py:43
  42.9 3.6 %collective-permute-start.4 = (bf16[1,2048]{1,0:T(2,128)(2,1)S(1)}, bf16[1,2048]{1,0:T(2,128)(2,1)S(1)}, u32[]{:S(2)}, u32[]{:S(2)}) collective-permute-start(bf16[1,2048]{1,0:T(2,128)(2,1)S(1)} %convert_element_type.266), channel_id=1, source_target_pairs={{0,1},{1,2},{2,3},{3,4},{4,5},{5,6},{6,7},{7,8},{8,9},{9,10},{10,1... | collective-permute-start | bytes 12296 | tf_op jit(solution)/shard_map/ppermute | solution.py:22
  47.4 1.8 collective-permute-start.6
  54.2 2.4 %collective-permute-start.7 = (f32[2,2,2048]{2,1,0:T(2,128)S(1)}, f32[2,2,2048]{2,1,0:T(2,128)S(1)}, u32[]{:S(2)}, u32[]{:S(2)}) collective-permute-start(f32[2,2,2048]{2,1,0:T(2,128)S(1)} %maximum_select_fusion.2), channel_id=1, source_target_pairs={{0,2},{1,3},{2,0},{3,1},{4,6},{5,7},{6,4},{7,5},{8,10},{9,11},{10,... | collective-permute-start | bytes 98312 | tf_op jit(solution)/shard_map/ppermute | solution.py:33
  60.1 2.2 %collective-permute-start.8 = (f32[4,2,2048]{2,1,0:T(2,128)S(1)}, f32[4,2,2048]{2,1,0:T(2,128)S(1)}, u32[]{:S(2)}, u32[]{:S(2)}) collective-permute-start(f32[4,2,2048]{2,1,0:T(2,128)S(1)} %maximum_select_fusion.1), channel_id=1, source_target_pairs={{0,4},{1,5},{2,6},{3,7},{4,0},{5,1},{6,2},{7,3},{8,12},{9,13},{10,... | collective-permute-start | bytes 196616 | tf_op jit(solution)/shard_map/ppermute | solution.py:33
  62.8 1.7 collective-permute-done.8
  72.2 1.7 fusion.155
  75.1 1.9 %copy.110 = f32[16,64,64,2]{1,0,3,2:T(8,128)} copy(f32[16,64,64,2]{2,0,1,3:T(8,128)S(1)} %get-tuple-element.67) | data formatting | bytes 1048576 | tf_op jit(solution)/shard_map/integer_pow | solution.py:182
  77.0 1.6 copy.111
  78.6 4.4 %fusion.164 = (f32[16,64,128]{2,1,0:T(8,128)S(1)}, f32[16,64,128]{2,1,0:T(8,128)}) fusion(f32[1,16,64,128]{3,2,1,0:T(8,128)} %param.22, f32[16,64,128]{2,1,0:T(8,128)S(1)} %copy.111, f32[1,16,64,128]{3,2,1,0:T(8,128)S(1)} %copy-done.2, f32[24,72,136]{2,1,0:T(8,128)S(1)} %select_maximum_fusion.6, f32[4,64,128]{2,1,0:T(8,128)} %copy-done.11, ...), kind=kLoop, calls=%fused_computation.321 | loop fusion | flops 5373952 | bytes 11796480 | tf_op jit(solution)/shard_map/add | solution.py:203
  85.7 5.2 %collective-permute-start.11 = (bf16[4,64,128]{2,1,0:T(8,128)(2,1)S(1)}, bf16[4,64,128]{2,1,0:T(8,128)(2,1)S(1)}, u32[]{:S(2)}, u32[]{:S(2)}) collective-permute-start(bf16[4,64,128]{2,1,0:T(8,128)(2,1)S(1)} %get-tuple-element.82), channel_id=1, source_target_pairs={{0,8},{1,9},{2,10},{3,11},{4,12},{5,13},{6,14},{7,15},{16,24},{17,... | collective-permute-start | bytes 196616 | tf_op jit(solution)/shard_map/ppermute | solution.py:43
  92.7 5.2 %collective-permute-done.12 = bf16[4,64,128]{2,1,0:T(8,128)(2,1)S(1)} collective-permute-done((bf16[4,64,128]{2,1,0:T(8,128)(2,1)S(1)}, bf16[4,64,128]{2,1,0:T(8,128)(2,1)S(1)}, u32[]{:S(2)}, u32[]{:S(2)}) %collective-permute-start.12) | collective-permute-done | bytes 65568 | tf_op jit(solution)/shard_map/ppermute | solution.py:43
  99.1 4.2 %multiply_add_fusion.2 = (f32[16,64,128]{2,1,0:T(8,128)S(1)}, f32[16,64,128]{2,1,0:T(8,128)}) fusion(f32[16,64,128]{2,1,0:T(8,128)} %copy-done.3, f32[16,64,128]{2,1,0:T(8,128)S(1)} %scatter-add.14, f32[1,16,64,128]{3,2,1,0:T(8,128)S(1)} %copy-done.2, f32[24,72,136]{2,1,0:T(8,128)S(1)} %select_maximum_fusion.4, f32[4,64,128]{2,1,0:T(8,128)} %copy-done.13, ...), kind=kLoop, calls=%fused_computation.326 | loop fusion | flops 5373952 | bytes 11272192 | tf_op jit(solution)/shard_map/add | solution.py:203
  106.1 1.6 collective-permute-start.13
  107.7 1.5 collective-permute-start.14
  110.0 1.5 gather_fusion
  111.5 3.3 %collective-permute-done.14 = bf16[4,64,128]{2,1,0:T(8,128)(2,1)S(1)} collective-permute-done((bf16[4,64,128]{2,1,0:T(8,128)(2,1)S(1)}, bf16[4,64,128]{2,1,0:T(8,128)(2,1)S(1)}, u32[]{:S(2)}, u32[]{:S(2)}) %collective-permute-start.14) | collective-permute-done | bytes 65568 | tf_op jit(solution)/shard_map/ppermute | solution.py:43
  116.0 4.2 %multiply_add_fusion.1 = (f32[16,64,128]{2,1,0:T(8,128)S(1)}, f32[16,64,128]{2,1,0:T(8,128)}) fusion(f32[16,64,128]{2,1,0:T(8,128)} %copy-done.3, f32[16,64,128]{2,1,0:T(8,128)S(1)} %scatter-add.14, f32[16,64,128]{2,1,0:T(8,128)S(1)} %scatter-add.15, f32[24,72,136]{2,1,0:T(8,128)S(1)} %select_maximum_fusion.2, f32[4,64,128]{2,1,0:T(8,128)} %copy-done.12, ...), kind=kLoop, calls=%fused_computation.325 | loop fusion | flops 5373952 | bytes 11272192 | tf_op jit(solution)/shard_map/add | solution.py:203
  123.0 2.2 %collective-permute-start.15 = (bf16[4,64,128]{2,1,0:T(8,128)(2,1)S(1)}, bf16[4,64,128]{2,1,0:T(8,128)(2,1)S(1)}, u32[]{:S(2)}, u32[]{:S(2)}) collective-permute-start(bf16[4,64,128]{2,1,0:T(8,128)(2,1)S(1)} %get-tuple-element.78), channel_id=1, source_target_pairs={{0,8},{1,9},{2,10},{3,11},{4,12},{5,13},{6,14},{7,15},{16,24},{17,... | collective-permute-start | bytes 196616 | tf_op jit(solution)/shard_map/ppermute | solution.py:43
  127.2 2.0 %copy.115 = f32[16,64,64,2]{1,0,3,2:T(8,128)} copy(f32[16,64,64,2]{2,0,1,3:T(8,128)S(1)} %copy-done.5) | data formatting | bytes 1048576 | tf_op jit(solution)/shard_map/mul | solution.py:215
  129.2 2.4 %copy.116 = f32[16,64,128]{2,1,0:T(8,128)} copy(f32[16,64,128]{1,0,2:T(8,128)} %bitcast.569) | data formatting | bytes 1048576 | tf_op jit(solution)/shard_map/mul | solution.py:215
  136.0 3.4 %fusion.158 = (f32[16,64,128]{2,1,0:T(8,128)}, f32[16,64,128]{2,1,0:T(8,128)S(1)}) fusion(f32[16,64,128]{2,1,0:T(8,128)S(1)} %copy-done.10, f32[16,64,128]{2,1,0:T(8,128)S(1)} %copy-done.9, f32[16,64,128]{2,1,0:T(8,128)S(1)} %copy-done.8, f32[16,64,128]{2,1,0:T(8,128)S(1)} %copy-done.7, bf16[4,1,16,64,128]{4,3,2,1,0:T(8,128)(2,1)S(1)} %copy-done.14, ...), kind=kLoop, calls=%fused_computation.310 | loop fusion | flops 6422528 | bytes 13369344 | tf_op jit(solution)/shard_map/mul | solution.py:215
  143.7 1.5 copy.117
  148.5 5.4 %collective-permute-start.18 = (f32[1,2048]{1,0:T(1,128)S(1)}, f32[1,2048]{1,0:T(1,128)S(1)}, u32[]{:S(2)}, u32[]{:S(2)}) collective-permute-start(f32[1,2048]{1,0:T(1,128)S(1)} %get-tuple-element.94), channel_id=1, source_target_pairs={{0,8},{1,9},{2,10},{3,11},{4,12},{5,13},{6,14},{7,15},{16,24},{17,... | collective-permute-start | bytes 24584 | tf_op jit(solution)/shard_map/ppermute | solution.py:43
  155.3 5.1 %collective-permute-done.17 = f32[1,2048]{1,0:T(1,128)S(1)} collective-permute-done((f32[1,2048]{1,0:T(1,128)S(1)}, f32[1,2048]{1,0:T(1,128)S(1)}, u32[]{:S(2)}, u32[]{:S(2)}) %collective-permute-start.17) | collective-permute-done | bytes 8224 | tf_op jit(solution)/shard_map/ppermute | solution.py:43
  160.5 2.1 %collective-permute-start.19 = (f32[4,1,2048]{2,0,1:T(4,128)S(1)}, f32[4,1,2048]{2,0,1:T(4,128)S(1)}, u32[]{:S(2)}, u32[]{:S(2)}) collective-permute-start(f32[4,1,2048]{2,0,1:T(4,128)S(1)} %select_bitcast_fusion), channel_id=1, source_target_pairs={{0,4},{1,5},{2,6},{3,7},{4,0},{5,1},{6,2},{7,3},{8,12},{9,13},{10,... | collective-permute-start | bytes 98312 | tf_op jit(solution)/shard_map/ppermute | solution.py:33
  162.6 1.9 collective-permute-done.19
  164.5 1.8 collective-permute-start.20
  166.4 2.0 %collective-permute-done.20 = f32[2,1,2048]{2,0,1:T(2,128)S(1)} collective-permute-done((f32[2,1,2048]{2,0,1:T(2,128)S(1)}, f32[2,1,2048]{2,0,1:T(2,128)S(1)}, u32[]{:S(2)}, u32[]{:S(2)}) %collective-permute-start.20) | collective-permute-done | bytes 16416 | tf_op jit(solution)/shard_map/ppermute | solution.py:33
  168.4 19.9 %all_gather.4 = f32[16,8,4,128]{3,1,2,0:T(8,128)S(1)} all-gather(f32[1,8,4,128]{3,1,2,0:T(8,128)S(1)} %broadcast_select_fusion.9), channel_id=1, replica_groups=mesh['groups'=2,'slab'=16] {'slab'}, dimensions={0}, use_global_device_ids=true | all-gather | bytes 278528 | tf_op jit(solution)/shard_map/all_gather | solution.py:213
  (257 shorter events, 57.3 us)
Async XLA Ops:
  0.6 32.1 %copy-start = (f32[8,4]{0,1:T(4,128)S(1)}, f32[8,4]{0,1:T(4,128)}, u32[]{:S(2)}) copy-start(f32[8,4]{0,1:T(4,128)} %param.25) | copy-start | bytes 388
  0.6 7.1 %copy-start.17 = (bf16[27,64,64]{2,1,0:T(8,128)(2,1)S(1)}, bf16[27,64,64]{2,1,0:T(8,128)(2,1)}, u32[]{:S(2)}) copy-start(bf16[27,64,64]{2,1,0:T(8,128)(2,1)} %param.19) | copy-start | bytes 663556
  0.7 5.6 %collective-permute-start.1 = (bf16[64,1,2048]{2,0,1:T(8,128)(2,1)}, bf16[64,1,2048]{2,0,1:T(8,128)(2,1)S(1)}, u32[]{:S(2)}, u32[]{:S(2)}) collective-permute-start(bf16[64,1,2048]{2,0,1:T(8,128)(2,1)} %param.18), channel_id=1, source_target_pairs={{1,0},{2,1},{3,2},{4,3},{5,4},{6,5},{7,6},{8,7},{9,8},{10,9},{11,1... | collective-permute-start | bytes 786440 | tf_op jit(solution)/shard_map/ppermute | solution.py:25
  2.1 4.4 %collective-permute-start = (bf16[64,1,2048]{2,0,1:T(8,128)(2,1)}, bf16[64,1,2048]{2,0,1:T(8,128)(2,1)S(1)}, u32[]{:S(2)}, u32[]{:S(2)}) collective-permute-start(bf16[64,1,2048]{2,0,1:T(8,128)(2,1)} %param.18), channel_id=1, source_target_pairs={{0,1},{1,2},{2,3},{3,4},{4,5},{5,6},{6,7},{7,8},{8,9},{9,10},{10,1... | collective-permute-start | bytes 786440 | tf_op jit(solution)/shard_map/ppermute | solution.py:22
  14.9 19.0 %copy-start.16 = (bf16[27,64,64]{2,1,0:T(8,128)(2,1)S(1)}, bf16[27,64,64]{2,1,0:T(8,128)(2,1)}, u32[]{:S(2)}) copy-start(bf16[27,64,64]{2,1,0:T(8,128)(2,1)} %param.20) | copy-start | bytes 663556
  15.2 18.2 %collective-permute-start.3 = (bf16[64,1,2048]{2,0,1:T(8,128)(2,1)S(1)}, bf16[64,1,2048]{2,0,1:T(8,128)(2,1)S(1)}, u32[]{:S(2)}, u32[]{:S(2)}) collective-permute-start(bf16[64,1,2048]{2,0,1:T(8,128)(2,1)S(1)} %bitcast.576), channel_id=1, source_target_pairs={{1,0},{2,1},{3,2},{4,3},{5,4},{6,5},{7,6},{8,7},{9,8},{10,9},{11,1... | collective-permute-start | bytes 786440 | tf_op jit(solution)/shard_map/ppermute | solution.py:25
  16.5 16.9 %collective-permute-start.2 = (bf16[64,1,2048]{2,0,1:T(8,128)(2,1)S(1)}, bf16[64,1,2048]{2,0,1:T(8,128)(2,1)S(1)}, u32[]{:S(2)}, u32[]{:S(2)}) collective-permute-start(bf16[64,1,2048]{2,0,1:T(8,128)(2,1)S(1)} %bitcast.577), channel_id=1, source_target_pairs={{0,1},{1,2},{2,3},{3,4},{4,5},{5,6},{6,7},{7,8},{8,9},{9,10},{10,1... | collective-permute-start | bytes 786440 | tf_op jit(solution)/shard_map/ppermute | solution.py:22
  25.7 34.2 %collective-permute-start.9 = (bf16[4,64,128]{2,1,0:T(8,128)(2,1)S(1)}, bf16[4,64,128]{2,1,0:T(8,128)(2,1)S(1)}, u32[]{:S(2)}, u32[]{:S(2)}) collective-permute-start(bf16[4,64,128]{2,1,0:T(8,128)(2,1)S(1)} %get-tuple-element.84), channel_id=1, source_target_pairs={{0,8},{1,9},{2,10},{3,11},{4,12},{5,13},{6,14},{7,15},{16,24},{17,... | collective-permute-start | bytes 196616 | tf_op jit(solution)/shard_map/ppermute | solution.py:43
  31.4 28.6 %collective-permute-start.10 = (bf16[4,64,128]{2,1,0:T(8,128)(2,1)S(1)}, bf16[4,64,128]{2,1,0:T(8,128)(2,1)S(1)}, u32[]{:S(2)}, u32[]{:S(2)}) collective-permute-start(bf16[4,64,128]{2,1,0:T(8,128)(2,1)S(1)} %get-tuple-element.85), channel_id=1, source_target_pairs={{8,0},{9,1},{10,2},{11,3},{12,4},{13,5},{14,6},{15,7},{24,16},{25,... | collective-permute-start | bytes 196616 | tf_op jit(solution)/shard_map/ppermute | solution.py:43
  40.7 5.9 %copy-start.18 = (s32[8,3]{0,1:T(4,128)S(1)}, s32[8,3]{0,1:T(4,128)}, u32[]{:S(2)}) copy-start(s32[8,3]{0,1:T(4,128)} %param.26) | copy-start | bytes 292
  40.7 16.0 %copy-start.21 = (s32[3]{0:T(128)S(1)}, s32[3]{0:T(128)}, u32[]{:S(2)}) copy-start(s32[3]{0:T(128)} %constant.246.clone.1) | copy-start | bytes 40
  40.7 21.6 %copy-start.2 = (f32[1,16,64,128]{3,2,1,0:T(8,128)S(1)}, f32[1,16,64,128]{3,2,1,0:T(8,128)}, u32[]{:S(2)}) copy-start(f32[1,16,64,128]{3,2,1,0:T(8,128)} %param.23) | copy-start | bytes 1572868
  41.6 5.0 %collective-permute-start.5 = (bf16[1,2048]{1,0:T(2,128)(2,1)S(1)}, bf16[1,2048]{1,0:T(2,128)(2,1)S(1)}, u32[]{:S(2)}, u32[]{:S(2)}) collective-permute-start(bf16[1,2048]{1,0:T(2,128)(2,1)S(1)} %convert_element_type.266), channel_id=1, source_target_pairs={{1,0},{2,1},{3,2},{4,3},{5,4},{6,5},{7,6},{8,7},{9,8},{10,9},{11,1... | collective-permute-start | bytes 12296 | tf_op jit(solution)/shard_map/ppermute | solution.py:25
  42.9 4.3 %collective-permute-start.4 = (bf16[1,2048]{1,0:T(2,128)(2,1)S(1)}, bf16[1,2048]{1,0:T(2,128)(2,1)S(1)}, u32[]{:S(2)}, u32[]{:S(2)}) collective-permute-start(bf16[1,2048]{1,0:T(2,128)(2,1)S(1)} %convert_element_type.266), channel_id=1, source_target_pairs={{0,1},{1,2},{2,3},{3,4},{4,5},{5,6},{6,7},{7,8},{8,9},{9,10},{10,1... | collective-permute-start | bytes 12296 | tf_op jit(solution)/shard_map/ppermute | solution.py:22
  47.4 6.8 %collective-permute-start.6 = (f32[1,2,2048]{2,1,0:T(2,128)S(1)}, f32[1,2,2048]{2,1,0:T(2,128)S(1)}, u32[]{:S(2)}, u32[]{:S(2)}) collective-permute-start(f32[1,2,2048]{2,1,0:T(2,128)S(1)} %pad_maximum_fusion.12), channel_id=1, source_target_pairs={{0,1},{1,0},{2,3},{3,2},{4,5},{5,4},{6,7},{7,6},{8,9},{9,8},{10,11... | collective-permute-start | bytes 49160 | tf_op jit(solution)/shard_map/ppermute | solution.py:33
  54.2 5.8 %collective-permute-start.7 = (f32[2,2,2048]{2,1,0:T(2,128)S(1)}, f32[2,2,2048]{2,1,0:T(2,128)S(1)}, u32[]{:S(2)}, u32[]{:S(2)}) collective-permute-start(f32[2,2,2048]{2,1,0:T(2,128)S(1)} %maximum_select_fusion.2), channel_id=1, source_target_pairs={{0,2},{1,3},{2,0},{3,1},{4,6},{5,7},{6,4},{7,5},{8,10},{9,11},{10,... | collective-permute-start | bytes 98312 | tf_op jit(solution)/shard_map/ppermute | solution.py:33
  60.0 5.3 %copy-start.11 = (f32[4,64,128]{2,1,0:T(8,128)}, f32[4,64,128]{2,1,0:T(8,128)S(1)}, u32[]{:S(2)}) copy-start(f32[4,64,128]{2,1,0:T(8,128)S(1)} %convert_element_type.271) | copy-start | bytes 393220
  60.1 4.5 %collective-permute-start.8 = (f32[4,2,2048]{2,1,0:T(2,128)S(1)}, f32[4,2,2048]{2,1,0:T(2,128)S(1)}, u32[]{:S(2)}, u32[]{:S(2)}) collective-permute-start(f32[4,2,2048]{2,1,0:T(2,128)S(1)} %maximum_select_fusion.1), channel_id=1, source_target_pairs={{0,4},{1,5},{2,6},{3,7},{4,0},{5,1},{6,2},{7,3},{8,12},{9,13},{10,... | collective-permute-start | bytes 196616 | tf_op jit(solution)/shard_map/ppermute | solution.py:33
  78.6 4.4 %copy-start.3 = (f32[16,64,128]{2,1,0:T(8,128)}, f32[16,64,128]{2,1,0:T(8,128)S(1)}, u32[]{:S(2)}) copy-start(f32[16,64,128]{2,1,0:T(8,128)S(1)} %copy.111) | copy-start | bytes 1572868
  85.7 7.1 %collective-permute-start.11 = (bf16[4,64,128]{2,1,0:T(8,128)(2,1)S(1)}, bf16[4,64,128]{2,1,0:T(8,128)(2,1)S(1)}, u32[]{:S(2)}, u32[]{:S(2)}) collective-permute-start(bf16[4,64,128]{2,1,0:T(8,128)(2,1)S(1)} %get-tuple-element.82), channel_id=1, source_target_pairs={{0,8},{1,9},{2,10},{3,11},{4,12},{5,13},{6,14},{7,15},{16,24},{17,... | collective-permute-start | bytes 196616 | tf_op jit(solution)/shard_map/ppermute | solution.py:43
  90.8 7.1 %collective-permute-start.12 = (bf16[4,64,128]{2,1,0:T(8,128)(2,1)S(1)}, bf16[4,64,128]{2,1,0:T(8,128)(2,1)S(1)}, u32[]{:S(2)}, u32[]{:S(2)}) collective-permute-start(bf16[4,64,128]{2,1,0:T(8,128)(2,1)S(1)} %get-tuple-element.83), channel_id=1, source_target_pairs={{8,0},{9,1},{10,2},{11,3},{12,4},{13,5},{14,6},{15,7},{24,16},{25,... | collective-permute-start | bytes 196616 | tf_op jit(solution)/shard_map/ppermute | solution.py:43
  106.1 5.3 %collective-permute-start.13 = (bf16[4,64,128]{2,1,0:T(8,128)(2,1)S(1)}, bf16[4,64,128]{2,1,0:T(8,128)(2,1)S(1)}, u32[]{:S(2)}, u32[]{:S(2)}) collective-permute-start(bf16[4,64,128]{2,1,0:T(8,128)(2,1)S(1)} %get-tuple-element.80), channel_id=1, source_target_pairs={{0,8},{1,9},{2,10},{3,11},{4,12},{5,13},{6,14},{7,15},{16,24},{17,... | collective-permute-start | bytes 196616 | tf_op jit(solution)/shard_map/ppermute | solution.py:43
  107.7 7.1 %collective-permute-start.14 = (bf16[4,64,128]{2,1,0:T(8,128)(2,1)S(1)}, bf16[4,64,128]{2,1,0:T(8,128)(2,1)S(1)}, u32[]{:S(2)}, u32[]{:S(2)}) collective-permute-start(bf16[4,64,128]{2,1,0:T(8,128)(2,1)S(1)} %get-tuple-element.81), channel_id=1, source_target_pairs={{8,0},{9,1},{10,2},{11,3},{12,4},{13,5},{14,6},{15,7},{24,16},{25,... | collective-permute-start | bytes 196616 | tf_op jit(solution)/shard_map/ppermute | solution.py:43
  120.1 7.1 %copy-start.5 = (f32[16,64,64,2]{2,0,1,3:T(8,128)S(1)}, f32[16,64,64,2]{2,0,1,3:T(8,128)}, u32[]{:S(2)}) copy-start(f32[16,64,64,2]{2,0,1,3:T(8,128)} %get-tuple-element.66) | copy-start | bytes 1572868
  123.0 11.6 %collective-permute-start.15 = (bf16[4,64,128]{2,1,0:T(8,128)(2,1)S(1)}, bf16[4,64,128]{2,1,0:T(8,128)(2,1)S(1)}, u32[]{:S(2)}, u32[]{:S(2)}) collective-permute-start(bf16[4,64,128]{2,1,0:T(8,128)(2,1)S(1)} %get-tuple-element.78), channel_id=1, source_target_pairs={{0,8},{1,9},{2,10},{3,11},{4,12},{5,13},{6,14},{7,15},{16,24},{17,... | collective-permute-start | bytes 196616 | tf_op jit(solution)/shard_map/ppermute | solution.py:43
  125.2 9.4 %collective-permute-start.16 = (bf16[4,64,128]{2,1,0:T(8,128)(2,1)S(1)}, bf16[4,64,128]{2,1,0:T(8,128)(2,1)S(1)}, u32[]{:S(2)}, u32[]{:S(2)}) collective-permute-start(bf16[4,64,128]{2,1,0:T(8,128)(2,1)S(1)} %get-tuple-element.79), channel_id=1, source_target_pairs={{8,0},{9,1},{10,2},{11,3},{12,4},{13,5},{14,6},{15,7},{24,16},{25,... | collective-permute-start | bytes 196616 | tf_op jit(solution)/shard_map/ppermute | solution.py:43
  147.8 41.8 %copy-start.1 = (f32[8,4]{0,1:T(4,128)S(1)}, f32[8,4]{0,1:T(4,128)}, u32[]{:S(2)}) copy-start(f32[8,4]{0,1:T(4,128)} %param.25) | copy-start | bytes 388
  148.5 6.8 %collective-permute-start.18 = (f32[1,2048]{1,0:T(1,128)S(1)}, f32[1,2048]{1,0:T(1,128)S(1)}, u32[]{:S(2)}, u32[]{:S(2)}) collective-permute-start(f32[1,2048]{1,0:T(1,128)S(1)} %get-tuple-element.94), channel_id=1, source_target_pairs={{0,8},{1,9},{2,10},{3,11},{4,12},{5,13},{6,14},{7,15},{16,24},{17,... | collective-permute-start | bytes 24584 | tf_op jit(solution)/shard_map/ppermute | solution.py:43
  153.9 6.4 %collective-permute-start.17 = (f32[1,2048]{1,0:T(1,128)S(1)}, f32[1,2048]{1,0:T(1,128)S(1)}, u32[]{:S(2)}, u32[]{:S(2)}) collective-permute-start(f32[1,2048]{1,0:T(1,128)S(1)} %get-tuple-element.95), channel_id=1, source_target_pairs={{8,0},{9,1},{10,2},{11,3},{12,4},{13,5},{14,6},{15,7},{24,16},{25,... | collective-permute-start | bytes 24584 | tf_op jit(solution)/shard_map/ppermute | solution.py:43
  160.5 4.0 %collective-permute-start.19 = (f32[4,1,2048]{2,0,1:T(4,128)S(1)}, f32[4,1,2048]{2,0,1:T(4,128)S(1)}, u32[]{:S(2)}, u32[]{:S(2)}) collective-permute-start(f32[4,1,2048]{2,0,1:T(4,128)S(1)} %select_bitcast_fusion), channel_id=1, source_target_pairs={{0,4},{1,5},{2,6},{3,7},{4,0},{5,1},{6,2},{7,3},{8,12},{9,13},{10,... | collective-permute-start | bytes 98312 | tf_op jit(solution)/shard_map/ppermute | solution.py:33
  164.5 3.8 %collective-permute-start.20 = (f32[2,1,2048]{2,0,1:T(2,128)S(1)}, f32[2,1,2048]{2,0,1:T(2,128)S(1)}, u32[]{:S(2)}, u32[]{:S(2)}) collective-permute-start(f32[2,1,2048]{2,0,1:T(2,128)S(1)} %broadcast_select_fusion.4), channel_id=1, source_target_pairs={{0,2},{1,3},{2,0},{3,1},{4,6},{5,7},{6,4},{7,5},{8,10},{9,11},{10,... | collective-permute-start | bytes 49160 | tf_op jit(solution)/shard_map/ppermute | solution.py:33
  168.4 20.6 %collective-permute-start.21 = (f32[1,1,2048]{2,0,1:T(1,128)S(1)}, f32[1,1,2048]{2,0,1:T(1,128)S(1)}, u32[]{:S(2)}, u32[]{:S(2)}) collective-permute-start(f32[1,1,2048]{2,0,1:T(1,128)S(1)} %broadcast_select_fusion.5), channel_id=1, source_target_pairs={{0,1},{1,0},{2,3},{3,2},{4,5},{5,4},{6,7},{7,6},{8,9},{9,8},{10,11... | collective-permute-start | bytes 24584 | tf_op jit(solution)/shard_map/ppermute | solution.py:33
  (13 other events, 19.8 us)
